TPU v7x, 32 devices: a whole 2x2x4 slice. The times are simulated.
32 devices in a mesh: row: 8 (over y, x, core), col: 4 (over z).
Axes of the slice: x: 2, y: 2, z: 4, core: 2. Of those that a mesh axis runs over, the one named last changes fastest.
Arguments:
- features: bfloat16 [6144, 256], P(('row', 'col')), may hold values from -6 to 6
- weight: bfloat16 [256, 256], replicated, may hold values from -0.375 to 0.375
- tiles: bfloat16 [8, 4, 256, 64, 128], P('row', 'col'), may hold values from -0.0546875 to 0.0546875
- tile_rows: int32 [8, 4, 512], P('row', 'col'), may hold values from 0 to 11
- tile_cols: int32 [8, 4, 512], P('row', 'col'), may hold values from 0 to 23
- counts: int32 [8, 4], P('row', 'col'), may hold values from 128 to 512, as said below
Outputs:
- output: bfloat16 [6144, 256], P(('row', 'col'))
Inputs may be any that keep to these rules, and one draw needn't show every extreme that they name: `counts`: some grid cell has exactly 512 live slots.
All inputs are finite; a program needn't handle non-finite values.
Results may differ from a plain program's by a relative error of at most 0.0049.
Values may be sent and summed in bfloat16 or wider, within the bound.
A program may use at most 64 MiB of HBM per device.

v0:
```python
import jax
import jax.numpy as jnp
from jax import lax
from jax.sharding import PartitionSpec as P

TILE = 64


def body(features, weight, tiles, tile_rows, tile_cols, counts):
    feature_width = weight.shape[1]
    product_rows = jnp.dot(features, weight, preferred_element_type=jnp.float32).astype(
        jnp.bfloat16
    )
    gathered = lax.all_gather(product_rows, "row", axis=0, tiled=True)
    column_table = gathered.reshape(gathered.shape[0] // TILE, TILE, feature_width)
    row_tiles = lax.axis_size("col") * features.shape[0] // TILE
    slot_count = tile_rows.shape[2]
    block_size = min(64, slot_count)
    half_block = block_size // 2
    passes = slot_count // block_size
    pair_list = tiles[0, 0]
    row_list = tile_rows[0, 0]
    col_list = tile_cols[0, 0]
    live_count = counts[0, 0]
    block_slots = jnp.arange(block_size, dtype=jnp.int32)

    def add_block(block_index, total):
        first = block_index * block_size
        pair_block = lax.dynamic_slice_in_dim(pair_list, block_index * half_block, half_block, 0)
        pair_block = pair_block.reshape(half_block, TILE, 2, TILE)
        row_block = lax.dynamic_slice_in_dim(row_list, first, block_size, 0)
        col_block = lax.dynamic_slice_in_dim(col_list, first, block_size, 0)
        picked = column_table[col_block].reshape(half_block, 2, TILE, feature_width)
        terms = jnp.einsum(
            "qajb,qjbf->qjaf", pair_block, picked, preferred_element_type=jnp.float32
        )
        terms = terms.reshape(block_size, TILE, feature_width)
        in_use = (first + block_slots < live_count).astype(jnp.float32)
        terms = terms * in_use[:, None, None]
        return total.at[row_block].add(terms)

    zero_total = jnp.zeros((row_tiles, TILE, feature_width), jnp.float32)
    total = lax.fori_loop(0, passes, add_block, zero_total)
    partial_value = total.reshape(row_tiles * TILE, feature_width)
    own_rows = lax.psum_scatter(partial_value, "col", scatter_dimension=0, tiled=True)
    return jnp.maximum(own_rows, 0.0).astype(jnp.bfloat16)


def solution(mesh):
    return jax.shard_map(
        body,
        mesh=mesh,
        in_specs=(
            P(("row", "col"), None),
            P(),
            P("row", "col", None, None, None),
            P("row", "col", None),
            P("row", "col", None),
            P("row", "col"),
        ),
        out_specs=P(("row", "col"), None),
        check_vma=False,
    )
```

profile of v0, /device:TPU:0, one launch (start us, length us, event | category | flops | bytes accessed | tf_op | source)
XLA Modules:
  0.0 206.8 jit_solution(1321664408388413104)
XLA Ops:
  8.5 12.9 %all_gather.3 = bf16[1536,256]{1,0:T(8,128)(2,1)} all-gather(bf16[192,256]{1,0:T(8,128)(2,1)S(1)} %convolution_convert_fusion), channel_id=1, replica_groups=mesh['row'=8,'col'=4] {'row'}, dimensions={0}, use_global_device_ids=true | all-gather | bytes 884736 | tf_op jit(solution)/shard_map/all_gather | solution.py:14
  21.5 152.2 %while.14 = (s32[]{:T(128)}, f32[12,64,256]{2,1,0:T(8,128)S(1)}, s32[512]{0:T(512)}, bf16[256,64,128]{2,1,0:T(8,128)(2,1)}, s32[512]{0:T(512)}, /*index=5*/bf16[...) while((s32[]{:T(128)}, f32[12,64,256]{2,1,0:T(8,128)S(1)}, ...), condition=%wide.region_2.0_spmd.clone, body=%wide.region_0.0_spmd.clone.sunk | while | flops 136316496 | bytes 34085360 | solution.py:43
  25.4 1.8 gather_fusion
  27.3 1.9 fusion.12
  29.2 2.5 %bitcast_multiply_fusion.2 = f32[64,64,256]{2,1,0:T(8,128)} fusion(f32[32,2,64,256]{3,2,1,0:T(8,128)S(1)} %fusion.12, f32[64]{0:T(128)S(1)} %compare_convert_fusion.2), kind=kLoop, calls=%fused_computation.3.clone.1 | loop fusion | flops 1048576 | bytes 8388864 | tf_op jit(solution)/shard_map/while/body/eval_jaxpr/mul | solution.py:39
  31.7 8.8 %scatter_fusion = f32[12,64,256]{2,1,0:T(8,128)S(1)} fusion(f32[12,64,256]{2,1,0:T(8,128)S(1)} %get-tuple-element.238, s32[64]{0:T(128)S(1)} %get-tuple-element.222, f32[64,64,256]{2,1,0:T(8,128)} %bitcast_multiply_fusion.2), kind=kCustom, calls=%fused_computation.1.clone.clone.1 | custom fusion | flops 1048576 | bytes 12583168 | tf_op jit(solution)/shard_map/while/body/eval_jaxpr/scatter-add | solution.py:40
  44.5 1.8 gather_fusion
  46.3 1.9 fusion.12
  48.2 2.5 %bitcast_multiply_fusion.2 = f32[64,64,256]{2,1,0:T(8,128)} fusion(f32[32,2,64,256]{3,2,1,0:T(8,128)S(1)} %fusion.12, f32[64]{0:T(128)S(1)} %compare_convert_fusion.2), kind=kLoop, calls=%fused_computation.3.clone.1 | loop fusion | flops 1048576 | bytes 8388864 | tf_op jit(solution)/shard_map/while/body/eval_jaxpr/mul | solution.py:39
  50.7 8.8 %scatter_fusion = f32[12,64,256]{2,1,0:T(8,128)S(1)} fusion(f32[12,64,256]{2,1,0:T(8,128)S(1)} %get-tuple-element.238, s32[64]{0:T(128)S(1)} %get-tuple-element.222, f32[64,64,256]{2,1,0:T(8,128)} %bitcast_multiply_fusion.2), kind=kCustom, calls=%fused_computation.1.clone.clone.1 | custom fusion | flops 1048576 | bytes 12583168 | tf_op jit(solution)/shard_map/while/body/eval_jaxpr/scatter-add | solution.py:40
  63.5 1.8 gather_fusion
  65.3 1.9 fusion.12
  67.2 2.5 %bitcast_multiply_fusion.2 = f32[64,64,256]{2,1,0:T(8,128)} fusion(f32[32,2,64,256]{3,2,1,0:T(8,128)S(1)} %fusion.12, f32[64]{0:T(128)S(1)} %compare_convert_fusion.2), kind=kLoop, calls=%fused_computation.3.clone.1 | loop fusion | flops 1048576 | bytes 8388864 | tf_op jit(solution)/shard_map/while/body/eval_jaxpr/mul | solution.py:39
  69.8 8.8 %scatter_fusion = f32[12,64,256]{2,1,0:T(8,128)S(1)} fusion(f32[12,64,256]{2,1,0:T(8,128)S(1)} %get-tuple-element.238, s32[64]{0:T(128)S(1)} %get-tuple-element.222, f32[64,64,256]{2,1,0:T(8,128)} %bitcast_multiply_fusion.2), kind=kCustom, calls=%fused_computation.1.clone.clone.1 | custom fusion | flops 1048576 | bytes 12583168 | tf_op jit(solution)/shard_map/while/body/eval_jaxpr/scatter-add | solution.py:40
  84.3 1.9 fusion.12
  86.2 2.5 %bitcast_multiply_fusion.2 = f32[64,64,256]{2,1,0:T(8,128)} fusion(f32[32,2,64,256]{3,2,1,0:T(8,128)S(1)} %fusion.12, f32[64]{0:T(128)S(1)} %compare_convert_fusion.2), kind=kLoop, calls=%fused_computation.3.clone.1 | loop fusion | flops 1048576 | bytes 8388864 | tf_op jit(solution)/shard_map/while/body/eval_jaxpr/mul | solution.py:39
  88.8 8.8 %scatter_fusion = f32[12,64,256]{2,1,0:T(8,128)S(1)} fusion(f32[12,64,256]{2,1,0:T(8,128)S(1)} %get-tuple-element.238, s32[64]{0:T(128)S(1)} %get-tuple-element.222, f32[64,64,256]{2,1,0:T(8,128)} %bitcast_multiply_fusion.2), kind=kCustom, calls=%fused_computation.1.clone.clone.1 | custom fusion | flops 1048576 | bytes 12583168 | tf_op jit(solution)/shard_map/while/body/eval_jaxpr/scatter-add | solution.py:40
  103.4 1.9 fusion.12
  105.3 2.5 %bitcast_multiply_fusion.2 = f32[64,64,256]{2,1,0:T(8,128)} fusion(f32[32,2,64,256]{3,2,1,0:T(8,128)S(1)} %fusion.12, f32[64]{0:T(128)S(1)} %compare_convert_fusion.2), kind=kLoop, calls=%fused_computation.3.clone.1 | loop fusion | flops 1048576 | bytes 8388864 | tf_op jit(solution)/shard_map/while/body/eval_jaxpr/mul | solution.py:39
  107.8 8.8 %scatter_fusion = f32[12,64,256]{2,1,0:T(8,128)S(1)} fusion(f32[12,64,256]{2,1,0:T(8,128)S(1)} %get-tuple-element.238, s32[64]{0:T(128)S(1)} %get-tuple-element.222, f32[64,64,256]{2,1,0:T(8,128)} %bitcast_multiply_fusion.2), kind=kCustom, calls=%fused_computation.1.clone.clone.1 | custom fusion | flops 1048576 | bytes 12583168 | tf_op jit(solution)/shard_map/while/body/eval_jaxpr/scatter-add | solution.py:40
  122.4 1.9 fusion.12
  124.3 2.5 %bitcast_multiply_fusion.2 = f32[64,64,256]{2,1,0:T(8,128)} fusion(f32[32,2,64,256]{3,2,1,0:T(8,128)S(1)} %fusion.12, f32[64]{0:T(128)S(1)} %compare_convert_fusion.2), kind=kLoop, calls=%fused_computation.3.clone.1 | loop fusion | flops 1048576 | bytes 8388864 | tf_op jit(solution)/shard_map/while/body/eval_jaxpr/mul | solution.py:39
  126.8 8.8 %scatter_fusion = f32[12,64,256]{2,1,0:T(8,128)S(1)} fusion(f32[12,64,256]{2,1,0:T(8,128)S(1)} %get-tuple-element.238, s32[64]{0:T(128)S(1)} %get-tuple-element.222, f32[64,64,256]{2,1,0:T(8,128)} %bitcast_multiply_fusion.2), kind=kCustom, calls=%fused_computation.1.clone.clone.1 | custom fusion | flops 1048576 | bytes 12583168 | tf_op jit(solution)/shard_map/while/body/eval_jaxpr/scatter-add | solution.py:40
  139.6 1.8 gather_fusion
  141.4 1.9 fusion.12
  143.3 2.5 %bitcast_multiply_fusion.2 = f32[64,64,256]{2,1,0:T(8,128)} fusion(f32[32,2,64,256]{3,2,1,0:T(8,128)S(1)} %fusion.12, f32[64]{0:T(128)S(1)} %compare_convert_fusion.2), kind=kLoop, calls=%fused_computation.3.clone.1 | loop fusion | flops 1048576 | bytes 8388864 | tf_op jit(solution)/shard_map/while/body/eval_jaxpr/mul | solution.py:39
  145.9 8.8 %scatter_fusion = f32[12,64,256]{2,1,0:T(8,128)S(1)} fusion(f32[12,64,256]{2,1,0:T(8,128)S(1)} %get-tuple-element.238, s32[64]{0:T(128)S(1)} %get-tuple-element.222, f32[64,64,256]{2,1,0:T(8,128)} %bitcast_multiply_fusion.2), kind=kCustom, calls=%fused_computation.1.clone.clone.1 | custom fusion | flops 1048576 | bytes 12583168 | tf_op jit(solution)/shard_map/while/body/eval_jaxpr/scatter-add | solution.py:40
  158.6 1.8 gather_fusion
  160.4 1.9 fusion.12
  162.4 2.5 %bitcast_multiply_fusion.2 = f32[64,64,256]{2,1,0:T(8,128)} fusion(f32[32,2,64,256]{3,2,1,0:T(8,128)S(1)} %fusion.12, f32[64]{0:T(128)S(1)} %compare_convert_fusion.2), kind=kLoop, calls=%fused_computation.3.clone.1 | loop fusion | flops 1048576 | bytes 8388864 | tf_op jit(solution)/shard_map/while/body/eval_jaxpr/mul | solution.py:39
  164.9 8.8 %scatter_fusion = f32[12,64,256]{2,1,0:T(8,128)S(1)} fusion(f32[12,64,256]{2,1,0:T(8,128)S(1)} %get-tuple-element.238, s32[64]{0:T(128)S(1)} %get-tuple-element.222, f32[64,64,256]{2,1,0:T(8,128)} %bitcast_multiply_fusion.2), kind=kCustom, calls=%fused_computation.1.clone.clone.1 | custom fusion | flops 1048576 | bytes 12583168 | tf_op jit(solution)/shard_map/while/body/eval_jaxpr/scatter-add | solution.py:40
  174.6 23.8 %reduce-scatter.2.cloned.1.call-done = f32[192,256]{1,0:T(8,128)} async-done(((f32[768,256]{1,0:T(8,128)}), f32[192,256]{1,0:T(8,128)}) %reduce-scatter.2.cloned.1.call-update) | async-done | bytes 196624 | tf_op jit(solution)/shard_map/reduce_scatter | solution.py:45
  (52 shorter events, 41.2 us)
Async XLA Ops:
  6.5 0.9 copy-start
  6.5 191.8 %reduce-scatter.2.cloned.1.call-start = ((), (), s32[]{:S(2)}) async-start(), calls=%async_computation.1 | async-start | bytes 983040 | tf_op jit(solution)/shard_map/reduce_scatter | solution.py:45
  173.7 0.9 copy-start.1
Sparse Core Ops, SparseCore 0:
  174.7 23.5 reduce-scatter.1
where the time goes:
time: 210 us; the launch traced here: 207 us
  other arithmetic  104 us (50%)
  local copies, waits for them, and re-layouts  36.1 us (17%)
  waiting for transfers between devices  23.8 us (11%)
  matrix products  16.3 us (8%)
  between operations  13.4 us (6%)
  blocking collectives  12.9 us (6%)
    scatter-add x8, other arithmetic, add_block(): return total.at[row_block].add(terms)  70.3 us
    reduce_scatter x1, waiting for transfers between devices, body(): lax.psum_scatter(partial_value, 'col', scatter_dimension=0, tiled=True)  23.8 us
    mul x8, other arithmetic, add_block(): terms = terms * in_use[:, None, None]  20.4 us
    dot_general x8, matrix products, add_block(): jnp.einsum('qajb,qjbf->qjaf', pair_block, picked, preferred_element_type=...  15.3 us
    gather x8, local copies, waits for them, and re-layouts, add_block(): picked = column_table[col_block].reshape(half_block, 2, TILE, feature_width)  14.5 us
    all_gather x1, blocking collectives, body(): gathered = lax.all_gather(product_rows, 'row', axis=0, tiled=True)  12.9 us
    reshape x8, local copies, waits for them, and re-layouts, add_block(): pair_block = pair_block.reshape(half_block, TILE, 2, TILE)  11.2 us
    dynamic_slice x8, local copies, waits for them, and re-layouts, add_block(): lax.dynamic_slice_in_dim(pair_list, block_index * half_block, half_block, 0)  8.66 us
  transfers between devices with their start and end apart: 1, of which 1 were waited for; matrix products, arithmetic and copies ran while one was open for 0% of the time, Pallas kernels for 0%

commit v1 on v0

--- a/solution.py
+++ b/solution.py
@@ -1,12 +1,176 @@
+import functools
+
 import jax
 import jax.numpy as jnp
 from jax import lax
+from jax.experimental import pallas as pl
+from jax.experimental.pallas import tpu as pltpu
 from jax.sharding import PartitionSpec as P
 
 TILE = 64
-
-
-def body(features, weight, tiles, tile_rows, tile_cols, counts):
+MESH = pl.DeviceIdType.MESH
+CHUNKS = 8
+GROUP = 4
+
+
+def densify_kernel(counts_ref, rows_ref, cols_ref, tiles_ref, dense_ref, tile_buf, acc, sems):
+    pairs = tiles_ref.shape[0]
+    per_chunk = pairs // CHUNKS
+    copies = []
+    for k in range(CHUNKS):
+        part = pl.ds(k * per_chunk, per_chunk)
+        copy = pltpu.make_async_copy(tiles_ref.at[part], tile_buf.at[part], sems.at[k])
+        copy.start()
+        copies.append(copy)
+    col_pairs = acc.shape[0]
+
+    @pl.loop(0, col_pairs)
+    def _(i):
+        acc[i] = jnp.zeros(acc.shape[1:], acc.dtype)
+
+    live = counts_ref[0]
+    live_pairs = (live + 1) // 2
+    lane_half = lax.broadcasted_iota(jnp.int32, (TILE, 2 * TILE), 1) // TILE
+    low = lane_half == 0
+
+    for k in range(CHUNKS):
+        copies[k].wait()
+        first = k * per_chunk
+        groups = jnp.clip((live_pairs - first + GROUP - 1) // GROUP, 0, per_chunk // GROUP)
+
+        @pl.loop(0, groups)
+        def _(g):
+            start = first + g * GROUP
+            work = []
+            for j in range(GROUP):
+                q = start + j
+                v = tile_buf[q].astype(jnp.float32)
+                swapped = pltpu.roll(v, TILE, 1)
+                work.append(jnp.where(low, v, swapped))
+                work.append(jnp.where(low, swapped, v))
+            for j in range(2 * GROUP):
+                p = 2 * start + j
+                r = rows_ref[p]
+                c = cols_ref[p]
+                half = jnp.where(p < live, c % 2, 2)
+                at = (c // 2, pl.ds(pl.multiple_of(r * TILE, TILE), TILE))
+                acc[at] += jnp.where(lane_half == half, work[j], 0.0)
+
+    @pl.loop(0, col_pairs)
+    def _(i):
+        dense_ref[i] = acc[i].astype(dense_ref.dtype)
+
+
+def densify(counts, rows, cols, tiles, row_tiles, col_tiles):
+    shape = (col_tiles // 2, row_tiles * TILE, 2 * TILE)
+    smem = pl.BlockSpec(memory_space=pltpu.SMEM)
+    return pl.pallas_call(
+        densify_kernel,
+        out_shape=jax.ShapeDtypeStruct(shape, jnp.bfloat16),
+        in_specs=[smem, smem, smem, pl.BlockSpec(memory_space=pl.ANY)],
+        out_specs=pl.BlockSpec(memory_space=pltpu.VMEM),
+        scratch_shapes=[
+            pltpu.VMEM(tiles.shape, tiles.dtype),
+            pltpu.VMEM(shape, jnp.float32),
+            pltpu.SemaphoreType.DMA((CHUNKS,)),
+        ],
+        compiler_params=pltpu.CompilerParams(vmem_limit_bytes=24 << 20),
+        cost_estimate=pl.CostEstimate(
+            flops=20_000_000_000, bytes_accessed=2 * tiles.size, transcendentals=0
+        ),
+    )(counts, rows, cols, tiles)
+
+
+def flip(index, mask, n):
+    out, bit = 0, 1
+    while bit < n:
+        have = (index // bit) % 2
+        out = out + bit * ((1 - have) if mask & bit else have)
+        bit *= 2
+    return out
+
+
+def combine_kernel(n_row, n_col, *refs):
+    pieces = refs[:n_row]
+    (weight_ref, dense_ref, out_ref, table, send, recv, send_sems, recv_sems) = refs[n_row:]
+    me_row, me = lax.axis_index("row"), lax.axis_index("col")
+    block = out_ref.shape[0]
+    barrier = pltpu.get_barrier_semaphore()
+    for j in range(1, n_col):
+        pl.semaphore_signal(
+            barrier, inc=1, device_id=(me_row, (me + j) % n_col), device_id_type=MESH
+        )
+    weight = weight_ref[...]
+    for s in range(n_row):
+        at = pl.multiple_of(flip(me_row, s, n_row) * block, block)
+        table[pl.ds(at, block)] = jnp.dot(
+            pieces[s][...], weight, preferred_element_type=jnp.float32
+        ).astype(table.dtype)
+    product = table[...]
+
+    def partial(owner):
+        at = pl.ds(pl.multiple_of(owner * block, block), block)
+        left = jnp.concatenate([dense_ref[i, at] for i in range(dense_ref.shape[0])], axis=1)
+        return jnp.dot(left, product, preferred_element_type=jnp.float32)
+
+    copies = []
+    for j in range(1, n_col):
+        peer = (me + j) % n_col
+        send[j - 1] = partial(peer).astype(send.dtype)
+        if j == 1:
+            pl.semaphore_wait(barrier, n_col - 1)
+        copy = pltpu.make_async_remote_copy(
+            src_ref=send.at[j - 1],
+            dst_ref=recv.at[j - 1],
+            send_sem=send_sems.at[j - 1],
+            recv_sem=recv_sems.at[j - 1],
+            device_id=(me_row, peer),
+            device_id_type=MESH,
+        )
+        copy.start()
+        copies.append(copy)
+    total = partial(me)
+    for j in range(n_col - 1):
+        copies[j].wait_recv()
+        total = total + recv[j].astype(jnp.float32)
+    out_ref[...] = jnp.maximum(total, 0.0).astype(out_ref.dtype)
+    for copy in copies:
+        copy.wait_send()
+
+
+def fast_body(n_row, n_col, features, weight, tiles, tile_rows, tile_cols, counts):
+    block, width = features.shape
+    pieces = [features]
+    for s in range(1, n_row):
+        pieces.append(lax.ppermute(features, "row", [(i, i ^ s) for i in range(n_row)]))
+    dense = densify(
+        counts.reshape(1),
+        tile_rows.reshape(-1),
+        tile_cols.reshape(-1),
+        tiles[0, 0],
+        n_col * block // TILE,
+        n_row * block // TILE,
+    )
+    vmem = pl.BlockSpec(memory_space=pltpu.VMEM)
+    return pl.pallas_call(
+        functools.partial(combine_kernel, n_row, n_col),
+        out_shape=jax.ShapeDtypeStruct((block, width), jnp.bfloat16),
+        in_specs=[vmem] * (n_row + 2),
+        out_specs=vmem,
+        scratch_shapes=[
+            pltpu.VMEM((n_row * block, width), jnp.bfloat16),
+            pltpu.VMEM((n_col - 1, block, width), jnp.bfloat16),
+            pltpu.VMEM((n_col - 1, block, width), jnp.bfloat16),
+            pltpu.SemaphoreType.DMA((n_col - 1,)),
+            pltpu.SemaphoreType.DMA((n_col - 1,)),
+        ],
+        compiler_params=pltpu.CompilerParams(
+            collective_id=0, has_side_effects=True, vmem_limit_bytes=24 << 20
+        ),
+    )(*pieces, weight, dense)
+
+
+def general_body(features, weight, tiles, tile_rows, tile_cols, counts):
     feature_width = weight.shape[1]
     product_rows = jnp.dot(features, weight, preferred_element_type=jnp.float32).astype(
         jnp.bfloat16
@@ -47,6 +211,10 @@
 
 
 def solution(mesh):
+    n_row, n_col = mesh.shape["row"], mesh.shape["col"]
+    power_of_two = n_row & (n_row - 1) == 0
+    fast = power_of_two and n_row * n_col <= 64
+    body = functools.partial(fast_body, n_row, n_col) if fast else general_body
     return jax.shard_map(
         body,
         mesh=mesh,

time: 210 us -> 35.1 us (0.17); the launches traced: 207 us -> 34.8 us
  other arithmetic: 104 us -> 0 us
  local copies, waits for them, and re-layouts: 36.1 us -> 4.2 us
  waiting for transfers between devices: 23.8 us -> 1.09 us
  Pallas kernels: 0 us -> 19.1 us
  matrix products: 16.3 us -> 0 us
  blocking collectives: 12.9 us -> 0 us
  between operations: 13.4 us -> 0.75 us
  starting transfers between devices: 0.01 us -> 9.66 us
    scatter-add x8 -> x0, other arithmetic: 70.3 us -> none  [add_block(): return total.at[row_block].add(terms)]
    reduce_scatter x1 -> x0, waiting for transfers between devices: 23.8 us -> none  [body(): lax.psum_scatter(partial_value, 'col', scatter_dimension=0, tiled=True)]
    mul x8 -> x0, other arithmetic: 20.4 us -> none  [add_block(): terms = terms * in_use[:, None, None]]
    pallas_call x0 -> x2, Pallas kernels: none -> 19.1 us  [the longest x1 11.3 us: fast_body(): pl.pallas_call(functools.partial(combine_kernel, n_row, n_col), out_shape...]
    dot_general x9 -> x0, matrix products: 16.3 us -> none  [the longest x8 15.3 us: add_block(): jnp.einsum('qajb,qjbf->qjaf', pair_block, picked, preferred_element_type=...]
    gather x8 -> x0, local copies, waits for them, and re-layouts: 14.5 us -> none  [add_block(): picked = column_table[col_block].reshape(half_block, 2, TILE, feature_width)]
    all_gather x1 -> x0, blocking collectives: 12.9 us -> none  [body(): gathered = lax.all_gather(product_rows, 'row', axis=0, tiled=True)]
    reshape x8 -> x0, local copies, waits for them, and re-layouts: 11.2 us -> none  [add_block(): pair_block = pair_block.reshape(half_block, TILE, 2, TILE)]
  transfers between devices with their start and end apart: 1 -> 7, of which waited for: 1 -> 1; matrix products, arithmetic and copies ran while one was open for 0% -> 0% of each run, Pallas kernels for 0% -> 22%
where the time goes in v1:
time: 35.1 us; the launch traced here: 34.8 us
  Pallas kernels  19.1 us (54%)
  starting transfers between devices  9.66 us (28%)
  local copies, waits for them, and re-layouts  4.2 us (12%)
  waiting for transfers between devices  1.09 us (3%)
  between operations  0.75 us (2%)
    pallas_call x1, Pallas kernels, fast_body(): pl.pallas_call(functools.partial(combine_kernel, n_row, n_col), out_shape...  11.3 us
    ppermute x7, starting transfers between devices, fast_body(): lax.ppermute(features, 'row', [(i, i ^ s) for i in range(n_row)])  9.66 us
    pallas_call x1, Pallas kernels, densify(): pl.pallas_call(densify_kernel, out_shape=jax.ShapeDtypeStruct(shape, jnp....  7.83 us
    unnamed x11, local copies, waits for them, and re-layouts  4.2 us
    ppermute x7, waiting for transfers between devices, fast_body(): lax.ppermute(features, 'row', [(i, i ^ s) for i in range(n_row)])  1.09 us
  transfers between devices with their start and end apart: 7, of which 1 were waited for; matrix products, arithmetic and copies ran while one was open for 0% of the time, Pallas kernels for 22%

profile of v1, /device:TPU:0, one launch (start us, length us, event | category | flops | bytes accessed | tf_op | source)
XLA Modules:
  0.0 34.8 jit_solution(5820472498666070203)
XLA Ops:
  0.0 3.9 %collective-permute-start.5 = (bf16[192,256]{1,0:T(8,128)(2,1)}, bf16[192,256]{1,0:T(8,128)(2,1)S(1)}, u32[]{:S(2)}, u32[]{:S(2)}) collective-permute-start(bf16[192,256]{1,0:T(8,128)(2,1)} %refs_0_.1), channel_id=1, source_target_pairs={{0,24},{4,28},{8,16},{12,20},{16,8},{20,12},{24,0},{28,4},{1,25},{... | collective-permute-start | bytes 294920 | tf_op jit(solution)/shard_map/ppermute | solution.py:145
  3.9 0.0 collective-permute-start.4
  3.9 1.2 %collective-permute-start.3 = (bf16[192,256]{1,0:T(8,128)(2,1)}, bf16[192,256]{1,0:T(8,128)(2,1)S(1)}, u32[]{:S(2)}, u32[]{:S(2)}) collective-permute-start(bf16[192,256]{1,0:T(8,128)(2,1)} %refs_0_.1), channel_id=1, source_target_pairs={{0,16},{4,20},{8,24},{12,28},{16,0},{20,4},{24,8},{28,12},{1,17},{... | collective-permute-start | bytes 294920 | tf_op jit(solution)/shard_map/ppermute | solution.py:145
  5.1 0.8 %collective-permute-start.2 = (bf16[192,256]{1,0:T(8,128)(2,1)}, bf16[192,256]{1,0:T(8,128)(2,1)S(1)}, u32[]{:S(2)}, u32[]{:S(2)}) collective-permute-start(bf16[192,256]{1,0:T(8,128)(2,1)} %refs_0_.1), channel_id=1, source_target_pairs={{0,12},{4,8},{8,4},{12,0},{16,28},{20,24},{24,20},{28,16},{1,13},{... | collective-permute-start | bytes 294920 | tf_op jit(solution)/shard_map/ppermute | solution.py:145
  5.9 1.5 %collective-permute-start.1 = (bf16[192,256]{1,0:T(8,128)(2,1)}, bf16[192,256]{1,0:T(8,128)(2,1)S(1)}, u32[]{:S(2)}, u32[]{:S(2)}) collective-permute-start(bf16[192,256]{1,0:T(8,128)(2,1)} %refs_0_.1), channel_id=1, source_target_pairs={{0,8},{4,12},{8,0},{12,4},{16,24},{20,28},{24,16},{28,20},{1,9},{5... | collective-permute-start | bytes 294920 | tf_op jit(solution)/shard_map/ppermute | solution.py:145
  8.0 0.0 collective-permute-done.5.refs_6_
  8.1 0.1 collective-permute-start
  8.1 1.1 %collective-permute-done.4.refs_5_ = bf16[192,256]{1,0:T(8,128)(2,1)S(1)} collective-permute-done((bf16[192,256]{1,0:T(8,128)(2,1)}, bf16[192,256]{1,0:T(8,128)(2,1)S(1)}, u32[]{:S(2)}, u32[]{:S(2)}) %collective-permute-start.4) | collective-permute-done | bytes 98336 | tf_op jit(solution)/shard_map/ppermute | solution.py:145
  9.2 2.2 %collective-permute-start.6 = (bf16[192,256]{1,0:T(8,128)(2,1)}, bf16[192,256]{1,0:T(8,128)(2,1)S(1)}, u32[]{:S(2)}, u32[]{:S(2)}) collective-permute-start(bf16[192,256]{1,0:T(8,128)(2,1)} %refs_0_.1), channel_id=1, source_target_pairs={{0,28},{4,24},{8,20},{12,16},{16,12},{20,8},{24,4},{28,0},{1,29},{... | collective-permute-start | bytes 294920 | tf_op jit(solution)/shard_map/ppermute | solution.py:145
  11.4 0.0 copy-start.2
  11.4 2.2 %copy-done.2 = bf16[1,1,256,64,128]{4,3,2,1,0:T(8,128)(2,1)S(1)} copy-done((bf16[1,1,256,64,128]{4,3,2,1,0:T(8,128)(2,1)S(1)}, bf16[1,1,256,64,128]{4,3,2,1,0:T(8,128)(2,1)}, u32[]{:S(2)}) %copy-start.2) | copy-done | bytes 4194328
  13.6 0.0 copy-start.3
  13.6 0.7 %copy-done.3 = s32[1,1,512]{2,1,0:T(1,128)S(1)} copy-done((s32[1,1,512]{2,1,0:T(1,128)S(1)}, s32[1,1,512]{2,1,0:T(1,128)}, u32[]{:S(2)}) %copy-start.3) | copy-done | bytes 2072
  14.3 0.0 copy-start.4
  14.3 0.7 %copy-done.4 = s32[1,1,512]{2,1,0:T(1,128)S(1)} copy-done((s32[1,1,512]{2,1,0:T(1,128)S(1)}, s32[1,1,512]{2,1,0:T(1,128)}, u32[]{:S(2)}) %copy-start.4) | copy-done | bytes 2072
  15.0 0.0 copy-start
  15.0 0.0 copy-start.1
  15.0 7.8 %shard_map.64.refs_9_ = bf16[12,768,128]{2,1,0:T(8,128)(2,1)S(1)} custom-call(s32[1]{0:T(128)} %bitcast.4.counts_ref, s32[512]{0:T(512)S(1)} %bitcast.6, s32[512]{0:T(512)S(1)} %bitcast.7, bf16[256,64,128]{2,1,0:T(8,128)(2,1)S(1)} %bitcast.5), custom_call_target="tpu_custom_call" | custom-call | flops 20000000000 | bytes 4194304 | tf_op jit(solution)/shard_map/pallas_call | solution.py:67
  22.8 0.0 collective-permute-done.3.refs_4_
  22.8 0.0 collective-permute-done.2.refs_3_
  22.8 0.0 collective-permute-done.1.refs_2_
  22.8 0.0 collective-permute-done.refs_1_
  22.8 0.0 collective-permute-done.6.refs_7_
  22.8 0.0 copy-done
  22.9 0.0 copy-done.1
  22.9 11.3 %shard_map.65 = bf16[192,256]{1,0:T(8,128)(2,1)S(1)} custom-call(bf16[192,256]{1,0:T(8,128)(2,1)S(1)} %copy-done.1, bf16[192,256]{1,0:T(8,128)(2,1)S(1)} %collective-permute-done.refs_1_, bf16[192,256]{1,0:T(8,128)(2,1)S(1)} %collective-permute-done.1.refs_2_, bf16[192,256]{1,0:T(8,128)(2,1)S(1)} %collective-permute-done.2.refs_3_, ...), custom_call_target="tpu_custom_call" | custom-call | tf_op jit(solution)/shard_map/pallas_call | solution.py:155
  34.1 0.6 %copy.9 = bf16[192,256]{1,0:T(8,128)(2,1)} copy(bf16[192,256]{1,0:T(8,128)(2,1)S(1)} %shard_map.65) | data formatting | bytes 196608
Async XLA Ops:
  0.0 8.0 %collective-permute-start.5 = (bf16[192,256]{1,0:T(8,128)(2,1)}, bf16[192,256]{1,0:T(8,128)(2,1)S(1)}, u32[]{:S(2)}, u32[]{:S(2)}) collective-permute-start(bf16[192,256]{1,0:T(8,128)(2,1)} %refs_0_.1), channel_id=1, source_target_pairs={{0,24},{4,28},{8,16},{12,20},{16,8},{20,12},{24,0},{28,4},{1,25},{... | collective-permute-start | bytes 294920 | tf_op jit(solution)/shard_map/ppermute | solution.py:145
  3.9 5.3 %collective-permute-start.4 = (bf16[192,256]{1,0:T(8,128)(2,1)}, bf16[192,256]{1,0:T(8,128)(2,1)S(1)}, u32[]{:S(2)}, u32[]{:S(2)}) collective-permute-start(bf16[192,256]{1,0:T(8,128)(2,1)} %refs_0_.1), channel_id=1, source_target_pairs={{0,20},{4,16},{8,28},{12,24},{16,4},{20,0},{24,12},{28,8},{1,21},{... | collective-permute-start | bytes 294920 | tf_op jit(solution)/shard_map/ppermute | solution.py:145
  3.9 18.9 %collective-permute-start.3 = (bf16[192,256]{1,0:T(8,128)(2,1)}, bf16[192,256]{1,0:T(8,128)(2,1)S(1)}, u32[]{:S(2)}, u32[]{:S(2)}) collective-permute-start(bf16[192,256]{1,0:T(8,128)(2,1)} %refs_0_.1), channel_id=1, source_target_pairs={{0,16},{4,20},{8,24},{12,28},{16,0},{20,4},{24,8},{28,12},{1,17},{... | collective-permute-start | bytes 294920 | tf_op jit(solution)/shard_map/ppermute | solution.py:145
  5.1 17.7 %collective-permute-start.2 = (bf16[192,256]{1,0:T(8,128)(2,1)}, bf16[192,256]{1,0:T(8,128)(2,1)S(1)}, u32[]{:S(2)}, u32[]{:S(2)}) collective-permute-start(bf16[192,256]{1,0:T(8,128)(2,1)} %refs_0_.1), channel_id=1, source_target_pairs={{0,12},{4,8},{8,4},{12,0},{16,28},{20,24},{24,20},{28,16},{1,13},{... | collective-permute-start | bytes 294920 | tf_op jit(solution)/shard_map/ppermute | solution.py:145
  5.9 16.9 %collective-permute-start.1 = (bf16[192,256]{1,0:T(8,128)(2,1)}, bf16[192,256]{1,0:T(8,128)(2,1)S(1)}, u32[]{:S(2)}, u32[]{:S(2)}) collective-permute-start(bf16[192,256]{1,0:T(8,128)(2,1)} %refs_0_.1), channel_id=1, source_target_pairs={{0,8},{4,12},{8,0},{12,4},{16,24},{20,28},{24,16},{28,20},{1,9},{5... | collective-permute-start | bytes 294920 | tf_op jit(solution)/shard_map/ppermute | solution.py:145
  8.1 14.8 %collective-permute-start = (bf16[192,256]{1,0:T(8,128)(2,1)}, bf16[192,256]{1,0:T(8,128)(2,1)S(1)}, u32[]{:S(2)}, u32[]{:S(2)}) collective-permute-start(bf16[192,256]{1,0:T(8,128)(2,1)} %refs_0_.1), channel_id=1, source_target_pairs={{0,4},{4,0},{8,12},{12,8},{16,20},{20,16},{24,28},{28,24},{1,5},{5... | collective-permute-start | bytes 294920 | tf_op jit(solution)/shard_map/ppermute | solution.py:145
  9.2 13.6 %collective-permute-start.6 = (bf16[192,256]{1,0:T(8,128)(2,1)}, bf16[192,256]{1,0:T(8,128)(2,1)S(1)}, u32[]{:S(2)}, u32[]{:S(2)}) collective-permute-start(bf16[192,256]{1,0:T(8,128)(2,1)} %refs_0_.1), channel_id=1, source_target_pairs={{0,28},{4,24},{8,20},{12,16},{16,12},{20,8},{24,4},{28,0},{1,29},{... | collective-permute-start | bytes 294920 | tf_op jit(solution)/shard_map/ppermute | solution.py:145
  11.4 2.2 %copy-start.2 = (bf16[1,1,256,64,128]{4,3,2,1,0:T(8,128)(2,1)S(1)}, bf16[1,1,256,64,128]{4,3,2,1,0:T(8,128)(2,1)}, u32[]{:S(2)}) copy-start(bf16[1,1,256,64,128]{4,3,2,1,0:T(8,128)(2,1)} %param.8) | copy-start | bytes 12582916
  13.6 0.7 %copy-start.3 = (s32[1,1,512]{2,1,0:T(1,128)S(1)}, s32[1,1,512]{2,1,0:T(1,128)}, u32[]{:S(2)}) copy-start(s32[1,1,512]{2,1,0:T(1,128)} %param.9) | copy-start | bytes 6148
  14.3 0.7 %copy-start.4 = (s32[1,1,512]{2,1,0:T(1,128)S(1)}, s32[1,1,512]{2,1,0:T(1,128)}, u32[]{:S(2)}) copy-start(s32[1,1,512]{2,1,0:T(1,128)} %param.10) | copy-start | bytes 6148
  15.0 7.9 %copy-start = (bf16[256,256]{1,0:T(8,128)(2,1)S(1)}, bf16[256,256]{1,0:T(8,128)(2,1)}, u32[]{:S(2)}) copy-start(bf16[256,256]{1,0:T(8,128)(2,1)} %refs_8_.1) | copy-start | bytes 393220
  15.0 7.9 %copy-start.1 = (bf16[192,256]{1,0:T(8,128)(2,1)S(1)}, bf16[192,256]{1,0:T(8,128)(2,1)}, u32[]{:S(2)}) copy-start(bf16[192,256]{1,0:T(8,128)(2,1)} %refs_0_.1) | copy-start | bytes 294916
